TPU v7x, 128 devices: a whole 4x4x4 slice. The times are simulated.
128 devices in a mesh: section: 16 (over y_hi, x, core), tp: 8 (over y_lo, z).
Axes of the slice: x: 4, y: 4 (y_hi: 2, y_lo: 2; y = y_hi * 2 + y_lo), z: 4, core: 2. Of those that a mesh axis runs over, the one named last changes fastest.
Arguments:
- activations: bfloat16 [16, 5, 1024, 8192], P('section', None, None, 'tp'), may hold values from -6 to 6
- cotangents: bfloat16 [16, 5, 1024, 2048], P('section', None, None, 'tp'), may hold values from -0.3984375 to 0.3984375
- section_code: int32 [16], replicated, may hold values from 0 to 15, each once
- boundaries: int32 [3, 17], replicated, may hold values from 0 to 16, as said below
- micro_counts: int32 [3], replicated, may hold values from 1 to 4, as said below
Outputs:
- layer_grads: float32 [16, 8192, 2048], P(None, 'tp', 'section')
Inputs may be any that keep to these rules, and one draw needn't show every extreme that they name: Row r lists replica r's boundaries: 0, then rising sums of its sections' lengths (4, 5, 7 sections), each 1 to 5 layers, ending at 16, then 16 repeated to the row's end; every replica has a section of exactly 5 layers. `micro_counts`: some replica has exactly 4.
All inputs are finite; a program needn't handle non-finite values.
Results may differ from a plain program's by a relative error of at most 0.0029.
Values may be sent and summed in bfloat16 or wider, within the bound.
A program may use at most 192 MiB of HBM per device.

v0:
```python
import jax
import jax.numpy as jnp
from jax import lax
from jax.sharding import PartitionSpec as P

MBT = 256


def per_device(activations, cotangents, section_code, boundaries, micro_counts):
    sections = lax.axis_size("section")
    start_second = sections // 4
    start_third = start_second + 5 * sections // 16
    slot_count = activations.shape[1]
    row_count = activations.shape[2]
    local_width = activations.shape[3]
    own_index = lax.axis_index("section")
    replica_all = (section_code >= start_second).astype(jnp.int32) + (
        section_code >= start_third
    ).astype(jnp.int32)
    start_all = jnp.where(
        replica_all == 0, 0, jnp.where(replica_all == 1, start_second, start_third)
    ).astype(jnp.int32)
    section_all = section_code - start_all
    lower_bound = boundaries[replica_all, section_all]
    upper_bound = boundaries[replica_all, section_all + 1]
    layer_of = lower_bound[:, None] + jnp.arange(slot_count, dtype=jnp.int32)[None, :]
    live_slot = layer_of < upper_bound[:, None]
    layer_ids = jnp.arange(sections, dtype=jnp.int32)[:, None, None]
    onehot = ((layer_of[None] == layer_ids) & live_slot[None]).astype(jnp.bfloat16)
    own_replica = replica_all[own_index]
    row_limit = MBT * micro_counts[own_replica]
    live_rows = (jnp.arange(row_count, dtype=jnp.int32) < row_limit)[None, :, None]
    masked = jnp.where(live_rows, cotangents[0], jnp.zeros((), jnp.bfloat16))
    inputs = activations[0]
    gathered = lax.all_gather(masked, "tp", axis=2, tiled=True)
    stacked_grads = jnp.einsum("jrd,jrc->jdc", inputs, gathered, preferred_element_type=jnp.float32)
    blocks = [stacked_grads[slot_index].astype(jnp.bfloat16) for slot_index in range(slot_count)]
    owned_cols = blocks[0].shape[1] // sections
    stacked = jnp.stack(blocks)[None]
    received = lax.all_to_all(stacked, "section", split_axis=3, concat_axis=0, tiled=True)
    flattened = received.reshape(sections * slot_count, local_width * owned_cols)
    summed = jnp.dot(
        onehot.reshape(sections, sections * slot_count),
        flattened,
        preferred_element_type=jnp.float32,
    )
    return summed.reshape(sections, local_width, owned_cols)


def solution(mesh):
    placed = (P("section", None, None, "tp"), P("section", None, None, "tp"), P(), P(), P())
    return jax.shard_map(
        per_device, mesh=mesh, in_specs=placed, out_specs=P(None, "tp", "section"), check_vma=False
    )
```

profile of v0, /device:TPU:0, one launch (start us, length us, event | category | flops | bytes accessed | tf_op | source)
XLA Modules:
  0.0 813.2 jit_solution(1321929355598143322)
XLA Ops:
  6.5 0.0 copy-start
  6.5 0.0 all-gather.2.cloned.1.call-start
  6.5 0.7 fusion.15
  7.2 0.6 dynamic_slice.6
  9.8 1.2 dynamic_slice.7
  11.7 3.0 copy.12
  14.7 1.7 bitcast_select_fusion
  16.3 0.0 all-gather.2.cloned.1.call-update
  16.4 212.7 %all-gather.2.cloned.1.call-done = bf16[5,1024,2048]{1,2,0:T(8,128)(2,1)} async-done(((bf16[5,1024,256]{1,2,0:T(8,128)(2,1)}), bf16[5,1024,2048]{1,2,0:T(8,128)(2,1)}) %all-gather.2.cloned.1.call-update) | async-done | bytes 20971536 | tf_op jit(solution)/shard_map/all_gather | solution.py:35
  229.1 31.2 %convert_bitcast_fusion = bf16[1,5,1024,2048]{2,3,1,0:T(8,128)(2,1)} fusion(bf16[5,1024,2048]{1,2,0:T(8,128)(2,1)} %all-gather.2.cloned.1.call-done, bf16[1,5,1024,1024]{3,2,1,0:T(8,128)(2,1)} %param.5), kind=kOutput, calls=%fused_computation.6 | convolution fusion | flops 21485322240 | bytes 52428800 | tf_op jit(solution)/shard_map/jrd,jrc->jdc/dot_general | solution.py:36
  260.2 23.9 %copy.13 = bf16[1,5,1024,2048]{2,1,0,3:T(8,128)(2,1)} copy(bf16[1,5,1024,2048]{2,3,1,0:T(8,128)(2,1)} %convert_bitcast_fusion) | data formatting | bytes 41943040 | tf_op jit(solution)/shard_map/broadcast_in_dim | solution.py:39
  284.2 6.6 all-to-all-start
  290.8 0.0 copy-done
  290.8 0.7 gather_fusion
  291.5 0.7 gather_fusion.1
  292.2 0.1 lt.43
  292.2 0.1 lt.44
  292.3 0.1 add.53
  292.4 0.1 add.54
  292.5 0.1 add.56
  292.6 446.8 %all-to-all-done = bf16[1,5,1024,2048]{2,1,0,3:T(8,128)(2,1)} async-done(((bf16[1,5,1024,2048]{2,1,0,3:T(8,128)(2,1)}), bf16[1,5,1024,2048]{2,1,0,3:T(8,128)(2,1)}, u32[]{:S(2)}, u32[]{:S(2)}) %all-to-all-start) | async-done | bytes 20971552 | tf_op jit(solution)/shard_map/all_to_all | solution.py:40
  739.5 40.6 %copy.14 = bf16[1,5,1024,16,128]{4,2,1,3,0:T(8,128)(2,1)} copy(bf16[1,5,1024,16,128]{2,1,4,3,0:T(8,128)(2,1)} %bitcast.7) | data formatting | bytes 41943040 | tf_op jit(solution)/shard_map/all_to_all | solution.py:40
  780.0 20.4 %fusion = f32[16,1024,128]{2,0,1:T(8,128)S(1)} fusion(s32[80]{0:T(128)S(1)} %get-tuple-element.6, pred[80]{0:T(512)(128)(4,1)S(1)} %get-tuple-element.5, bf16[10,8,1024,128]{3,2,1,0:T(8,128)(2,1)} %bitcast.36), kind=kOutput, calls=%fused_computation.3 | convolution fusion | flops 335546880 | bytes 29360528 | tf_op jit(solution)/shard_map/dot_general | solution.py:42
  800.4 6.0 copy.16
  (3 shorter events, 0.0 us)
Async XLA Ops:
  6.5 284.2 %copy-start = (s32[3,17]{1,0:T(4,128)S(1)}, s32[3,17]{1,0:T(4,128)}, u32[]{:S(2)}) copy-start(s32[3,17]{1,0:T(4,128)} %param.8) | copy-start | bytes 616
  6.5 222.5 %all-gather.2.cloned.1.call-start = ((), (), s32[]{:S(2)}) async-start(), calls=%async_computation.1 | async-start | bytes 23592960 | tf_op jit(solution)/shard_map/all_gather | solution.py:35
  284.2 455.3 %all-to-all-start = ((bf16[1,5,1024,2048]{2,1,0,3:T(8,128)(2,1)}), bf16[1,5,1024,2048]{2,1,0,3:T(8,128)(2,1)}, u32[]{:S(2)}, u32[]{:S(2)}) async-start(bf16[1,5,1024,2048]{2,1,0,3:T(8,128)(2,1)} %copy.13), calls=%async_computation | async-start | bytes 67108864 | tf_op jit(solution)/shard_map/all_to_all | solution.py:40
Sparse Core Ops, SparseCore 0:
  16.5 212.5 all-gather.1
where the time goes:
time: 816 us; the launch traced here: 813 us
  waiting for transfers between devices  660 us (81%)
  local copies, waits for them, and re-layouts  77.1 us (9%)
  matrix products  51.6 us (6%)
  between operations  16 us (2%)
    all_to_all x1, waiting for transfers between devices, per_device(): lax.all_to_all(stacked, 'section', split_axis=3, concat_axis=0, tiled=True)  447 us
    all_gather x1, waiting for transfers between devices, per_device(): gathered = lax.all_gather(masked, 'tp', axis=2, tiled=True)  213 us
    all_to_all x1, local copies, waits for them, and re-layouts, per_device(): lax.all_to_all(stacked, 'section', split_axis=3, concat_axis=0, tiled=True)  40.6 us
    dot_general x1, matrix products, per_device(): jnp.einsum('jrd,jrc->jdc', inputs, gathered, preferred_element_type=jnp.f...  31.2 us
    broadcast_in_dim x1, local copies, waits for them, and re-layouts, per_device(): stacked = jnp.stack(blocks)[None]  23.9 us
    dot_general x1, matrix products, per_device(): jnp.dot(onehot.reshape(sections, sections * slot_count), flattened, prefe...  20.4 us
  transfers between devices with their start and end apart: 2, of which 2 were waited for; matrix products, arithmetic and copies ran while one was open for 0% of the time, Pallas kernels for 0%

commit v1 on v0

v1 whole, which is shorter than its diff:
```python
import functools

import jax
import jax.numpy as jnp
from jax import lax
from jax.experimental import pallas as pl
from jax.experimental.pallas import tpu as pltpu
from jax.sharding import PartitionSpec as P

MBT = 256
MESH = pl.DeviceIdType.MESH
SLOTS = 5
UNITS = 2 * SLOTS
ROWS = 1024
WIDTH = 1024
LAYERS = 16
CHUNKS = 8
CROWS = 512 // CHUNKS


def place():
    section = lax.axis_index("section")
    tp = lax.axis_index("tp")
    return section // 8, (section // 2) % 4, section % 2, tp // 4, tp % 4


def device(yh, x, c, yl, z):
    return ((yh * 4 + x) * 2 + c, yl * 4 + z)


def greet(peers):
    barrier = pltpu.get_barrier_semaphore()
    for peer in peers:
        pl.semaphore_signal(barrier, inc=1, device_id=peer, device_id_type=MESH)
    pl.semaphore_wait(barrier, len(peers))


def gather_multiply(
    c_ref, a_ref, kept, recv, a2, cbuf, abuf, stk, sts,
    loc_sem, cs_sem, cr_sem, as_sem, ar_sem, ms_sem, mr_sem, al_sem, k_sem, ps_sem, pr_sem,
):
    yh, x, c, yl, z = place()
    xa = x + 1 - 2 * (x % 2)
    xb = 3 - x
    mate = device(yh, x, 1 - c, yl, z)
    ypeer = device(yh, x, c, 1 - yl, z)
    zplus = device(yh, x, c, yl, (z + 1) % 4)
    zminus = device(yh, x, c, yl, (z + 3) % 4)
    peer_a = device(yh, xa, c, yl, z)
    peer_b = device(yh, xb, c, yl, z)
    greet((mate, ypeer, zplus, zminus, peer_a, peer_b))
    turn = 1 + 2 * (x % 2)

    def column(yy, zz):
        place_x = ((zz % 4 - x + 4) * turn) % 4
        place_y = (yy - yh + 2) % 2
        return pl.multiple_of((place_x * 2 + place_y) * 128, 128)

    def shard(s, yy, zz, row=0, rows=ROWS):
        return cbuf.at[s, pl.ds(row, rows), pl.ds(column(yy, zz), 128)]

    def own_c(j):
        return pltpu.make_async_copy(
            c_ref.at[j, :, pl.ds(pl.multiple_of(c * 128, 128), 128)], shard(2 * j, yl, z), loc_sem.at[j]
        )

    def mate_c(j):
        return pltpu.make_async_remote_copy(
            c_ref.at[j, :, pl.ds(pl.multiple_of((1 - c) * 128, 128), 128)],
            shard(2 * j + 1, yl, z), cs_sem.at[j], cr_sem.at[j], device_id=mate, device_id_type=MESH,
        )

    def mate_a(j):
        return pltpu.make_async_remote_copy(
            a_ref.at[j], a2.at[j], as_sem.at[j], ar_sem.at[j], device_id=mate, device_id_type=MESH
        )

    half = ROWS // 2

    def message(kind, s):
        if kind <= 2:
            ref, target = shard(s, yl, z), (ypeer, zplus, zminus)[kind]
        elif kind <= 4:
            ref, target = shard(s, 1 - yl, z), (zplus, zminus)[kind - 3]
        elif kind == 5:
            ref, target = shard(s, yl, z + 3, 0, half), zplus
        elif kind == 6:
            ref, target = shard(s, yl, z + 1, half, half), zminus
        else:
            ref, target = shard(s, yl, z + 2), ypeer
        return pltpu.make_async_remote_copy(
            ref, ref, ms_sem.at[kind, s], mr_sem.at[kind, s], device_id=target, device_id_type=MESH
        )

    def load_own(j):
        return pltpu.make_async_copy(a_ref.at[j], abuf.at[0], al_sem.at[0])

    def load_mate(j):
        return pltpu.make_async_copy(a2.at[j], abuf.at[1], al_sem.at[1])

    def keep(s, b):
        return pltpu.make_async_copy(stk.at[b], kept.at[s], k_sem.at[b])

    def swap(s, b, h):
        return pltpu.make_async_remote_copy(
            sts.at[b, h], recv.at[s, h], ps_sem.at[b, h], pr_sem.at[s, h],
            device_id=(peer_a, peer_b)[h], device_id_type=MESH,
        )

    for j in range(SLOTS):
        own_c(j).start()
        mate_c(j).start()
    load_own(0).start()
    for j in range(SLOTS):
        mate_a(j).start()

    def compute(s, b):
        j = s // 2
        if b == 0:
            mate_a(j).wait_recv()
            load_mate(j).start()
            load_own(j).wait()
        else:
            @pl.when(j < SLOTS - 1)
            def _():
                load_own(j + 1).start()

            load_mate(j).wait()

        @pl.when(j > 0)
        def _():
            keep(s - 2, b).wait()
            swap(s - 2, b, 0).wait_send()
            swap(s - 2, b, 1).wait_send()

        for h in range(2):
            @pl.loop(0, 2)
            def _(tile):
                at = pl.multiple_of(tile * 256, 256)
                block = lax.dot_general(
                    abuf[b, :, pl.ds(h * 512 + at, 256)], cbuf[s],
                    (((0,), (0,)), ((), ())), preferred_element_type=jnp.float32,
                ).astype(jnp.bfloat16)
                rows = pl.ds(at, 256)
                if h == 0:
                    sts[b, 0, rows, :] = block[:, 256:768]
                    stk[b, 0, rows, 0:256] = block[:, 0:256]
                    stk[b, 0, rows, 256:512] = block[:, 768:1024]
                else:
                    sts[b, 1, rows, 0:256] = block[:, 768:1024]
                    sts[b, 1, rows, 256:512] = block[:, 512:768]
                    stk[b, 1, rows, :] = block[:, 0:512]

            swap(s, b, h).start()
        keep(s, b).start()

    @pl.loop(0, UNITS + 3)
    def _(it):
        @pl.when(it < UNITS)
        def _():
            @pl.when(it % 2 == 0)
            def _():
                own_c(it // 2).wait()

            @pl.when(it % 2 == 1)
            def _():
                mate_c(it // 2).wait_recv()

            for kind in (0, 1, 2):
                message(kind, it).start()

        @pl.when((it >= 1) & (it < UNITS + 1))
        def _():
            s = it - 1
            message(0, s).wait_recv()
            message(3, s).start()
            message(4, s).start()
            message(1, s).wait_recv()
            message(5, s).start()
            message(2, s).wait_recv()
            message(6, s).start()

        @pl.when((it >= 2) & (it < UNITS + 2))
        def _():
            s = it - 2
            message(5, s).wait_recv()
            message(6, s).wait_recv()
            message(7, s).start()

        @pl.when(it >= 3)
        def _():
            s = it - 3
            message(3, s).wait_recv()
            message(4, s).wait_recv()
            message(7, s).wait_recv()

            @pl.when(s % 2 == 0)
            def _():
                compute(s, 0)

            @pl.when(s % 2 == 1)
            def _():
                compute(s, 1)

    for b in range(2):
        s = UNITS - 2 + b
        keep(s, b).wait()
        swap(s, b, 0).wait_send()
        swap(s, b, 1).wait_send()
    for j in range(SLOTS):
        mate_c(j).wait_send()
        mate_a(j).wait_send()

    @pl.loop(0, UNITS)
    def _(s):
        for kind in range(8):
            message(kind, s).wait_send()
        for h in range(2):
            swap(s, 0, h).wait_recv()


def merge(
    slot_of, weight_of, kept, recv, out, ld_even, ld_odd, p2k, p2s, p2r, p3k, p3s, p3r, ost,
    ld_sem, s2_sem, r2_sem, s3_sem, r3_sem, o_sem,
):
    yh, x, c, yl, z = place()
    peer_a = device(yh, x + 1 - 2 * (x % 2), c, yl, z)
    peer_b = device(yh, 3 - x, c, yl, z)
    peer_y = device(1 - yh, x, c, yl, z)
    greet((peer_a, peer_b, peer_y))

    ld = (ld_even, ld_odd)

    def loads(n, b):
        rows = pl.ds(pl.multiple_of(n * CROWS, CROWS), CROWS)
        return [
            pltpu.make_async_copy(source.at[:, h, rows, :], ld[b].at[h, pl.ds(g * UNITS, UNITS)], ld_sem.at[b, h, g])
            for h in range(2)
            for g, source in enumerate((kept, recv))
        ]

    def send_x(n, b, h):
        return pltpu.make_async_remote_copy(
            p2s.at[b, h], p2r.at[n, h], s2_sem.at[b, h], r2_sem.at[n, h],
            device_id=(peer_b, peer_a)[h], device_id_type=MESH,
        )

    def send_y(n, b):
        return pltpu.make_async_remote_copy(
            p3s.at[b], p3r.at[n], s3_sem.at[b], r3_sem.at[n], device_id=peer_y, device_id_type=MESH
        )

    def store(n, b, h):
        return pltpu.make_async_copy(
            ost.at[b, h], out.at[:, pl.ds(pl.multiple_of(h * 512 + n * CROWS, CROWS), CROWS), :], o_sem.at[b, h]
        )

    for load in loads(0, 0):
        load.start()

    def first(n, b):
        @pl.when(n + 1 < CHUNKS)
        def _():
            for load in loads(n + 1, 1 - b):
                load.start()

        for load in loads(n, b):
            load.wait()
        for h in range(2):
            @pl.when(n >= 2)
            def _():
                send_x(n - 2, b, h).wait_send()

            @pl.loop(0, LAYERS)
            def _(layer):
                total = None
                for q in range(4):
                    at = (h * LAYERS + layer) * 4 + q
                    term = ld[b][h, slot_of[at]].astype(jnp.float32) * weight_of[at]
                    total = term if total is None else total + term
                p2k[b, h, layer] = total[:, 0:256]
                p2s[b, h, layer] = total[:, 256:512].astype(jnp.bfloat16)

            send_x(n, b, h).start()

    def second(n, b):
        @pl.when(n >= 2)
        def _():
            send_y(n - 2, b).wait_send()

        for h in range(2):
            send_x(n, b, h).wait_recv()

            @pl.loop(0, LAYERS)
            def _(layer):
                total = p2k[b, h, layer] + p2r[n, h, layer].astype(jnp.float32)
                p3k[b, h, layer] = total[:, 0:128]
                p3s[b, h, layer] = total[:, 128:256].astype(jnp.bfloat16)

        send_y(n, b).start()

    def third(n, b):
        send_y(n, b).wait_recv()
        for h in range(2):
            @pl.when(n >= 2)
            def _():
                store(n - 2, b, h).wait()

            @pl.loop(0, LAYERS)
            def _(layer):
                ost[b, h, layer] = p3k[b, h, layer] + p3r[n, h, layer].astype(jnp.float32)

            store(n, b, h).start()

    @pl.loop(0, CHUNKS // 2 + 1)
    def _(it):
        for b in range(2):
            n = it * 2 + b

            @pl.when(n < CHUNKS)
            def _():
                first(n, b)

            @pl.when((n >= 1) & (n < CHUNKS + 1))
            def _():
                second(n - 1, 1 - b)

            @pl.when(n >= 2)
            def _():
                third(n - 2, b)

    for b in range(2):
        n = CHUNKS - 2 + b
        send_y(n, b).wait_send()
        for h in range(2):
            send_x(n, b, h).wait_send()
            store(n, b, h).wait()


def tables(section_code, boundaries):
    replica = (section_code >= 4).astype(jnp.int32) + (section_code >= 9).astype(jnp.int32)
    part = section_code - jnp.where(replica == 0, 0, jnp.where(replica == 1, 4, 9))
    low = boundaries[replica, part]
    high = boundaries[replica, part + 1]
    own = lax.axis_index("section")
    x = (own // 2) % 4
    base = own - 2 * x
    mate = own + 1 - 2 * (own % 2)
    slots, weights = [], []
    layers = jnp.arange(LAYERS, dtype=jnp.int32)
    for partner_x in (x + 1 - 2 * (x % 2), 3 - x):
        partner = base + 2 * partner_x
        partner_mate = partner + 1 - 2 * (partner % 2)
        for q, section in enumerate((own, mate, partner, partner_mate)):
            slot = layers - low[section]
            live = (slot >= 0) & (layers < high[section])
            slots.append(jnp.where(live, 2 * slot + (q % 2) + UNITS * (q // 2), 0))
            weights.append(live.astype(jnp.float32))
    order = lambda v: jnp.stack(v).reshape(2, 4, LAYERS).transpose(0, 2, 1).reshape(-1)
    return replica, order(slots).astype(jnp.int32), order(weights)


def per_device(activations, cotangents, section_code, boundaries, micro_counts):
    replica, slot_of, weight_of = tables(section_code, boundaries)
    row_limit = MBT * micro_counts[replica[lax.axis_index("section")]]
    live_rows = (jnp.arange(ROWS, dtype=jnp.int32) < row_limit)[None, :, None]
    masked = jnp.where(live_rows, cotangents[0], jnp.zeros((), jnp.bfloat16))
    any_spec = pl.BlockSpec(memory_space=pl.ANY)
    smem_spec = pl.BlockSpec(memory_space=pltpu.SMEM)
    dma = pltpu.SemaphoreType.DMA
    blocks = jax.ShapeDtypeStruct((UNITS, 2, 512, 512), jnp.bfloat16)
    kept, recv, _ = pl.pallas_call(
        gather_multiply,
        name="gather_multiply",
        out_shape=(blocks, blocks, jax.ShapeDtypeStruct((SLOTS, ROWS, WIDTH), jnp.bfloat16)),
        in_specs=[any_spec] * 2,
        out_specs=(any_spec,) * 3,
        scratch_shapes=[
            pltpu.VMEM((UNITS, ROWS, 1024), jnp.bfloat16),
            pltpu.VMEM((2, ROWS, WIDTH), jnp.bfloat16),
            pltpu.VMEM((2, 2, 512, 512), jnp.bfloat16),
            pltpu.VMEM((2, 2, 512, 512), jnp.bfloat16),
            dma((SLOTS,)), dma((SLOTS,)), dma((SLOTS,)), dma((SLOTS,)), dma((SLOTS,)),
            dma((8, UNITS)), dma((8, UNITS)), dma((2,)), dma((2,)), dma((2, 2)), dma((UNITS, 2)),
        ],
        compiler_params=pltpu.CompilerParams(
            collective_id=0, has_side_effects=True, vmem_limit_bytes=56 << 20
        ),
    )(masked, activations[0])
    return pl.pallas_call(
        merge,
        name="merge",
        out_shape=jax.ShapeDtypeStruct((LAYERS, WIDTH, 128), jnp.float32),
        in_specs=[smem_spec, smem_spec, any_spec, any_spec],
        out_specs=any_spec,
        scratch_shapes=[
            pltpu.VMEM((2, 2 * UNITS, CROWS, 512), jnp.bfloat16),
            pltpu.VMEM((2, 2 * UNITS, CROWS, 512), jnp.bfloat16),
            pltpu.VMEM((2, 2, LAYERS, CROWS, 256), jnp.float32),
            pltpu.VMEM((2, 2, LAYERS, CROWS, 256), jnp.bfloat16),
            pltpu.VMEM((CHUNKS, 2, LAYERS, CROWS, 256), jnp.bfloat16),
            pltpu.VMEM((2, 2, LAYERS, CROWS, 128), jnp.float32),
            pltpu.VMEM((2, 2, LAYERS, CROWS, 128), jnp.bfloat16),
            pltpu.VMEM((CHUNKS, 2, LAYERS, CROWS, 128), jnp.bfloat16),
            pltpu.VMEM((2, 2, LAYERS, CROWS, 128), jnp.float32),
            dma((2, 2, 2)), dma((2, 2)), dma((CHUNKS, 2)), dma((2,)), dma((CHUNKS,)), dma((2, 2)),
        ],
        compiler_params=pltpu.CompilerParams(
            collective_id=1, has_side_effects=True, vmem_limit_bytes=56 << 20
        ),
    )(slot_of, weight_of, kept, recv)


def solution(mesh):
    placed = (P("section", None, None, "tp"), P("section", None, None, "tp"), P(), P(), P())
    return jax.shard_map(
        per_device, mesh=mesh, in_specs=placed, out_specs=P(None, "tp", "section"), check_vma=False
    )
```

time: 816 us -> 326 us (0.40)
  waiting for transfers between devices: 660 us -> 0 us
  Pallas kernels: 0 us -> 290 us
  local copies, waits for them, and re-layouts: 77.1 us -> 13.1 us
  matrix products: 51.6 us -> 0 us
  other arithmetic: 2.36 us -> 19.1 us
  between operations: 16 us -> 2.71 us
    all_to_all x1 -> x0, waiting for transfers between devices: 447 us -> none  [per_device(): lax.all_to_all(stacked, 'section', split_axis=3, concat_axis=0, tiled=True)]
    pallas_call x0 -> x2, Pallas kernels: none -> 290 us  [the longest x1 181 us: per_device(): pl.pallas_call(gather_multiply, name='gather_multiply', out_shape=(blocks...]
    all_gather x1 -> x0, waiting for transfers between devices: 213 us -> none  [per_device(): gathered = lax.all_gather(masked, 'tp', axis=2, tiled=True)]
    dot_general x2 -> x0, matrix products: 51.6 us -> none  [the longest x1 31.2 us: per_device(): jnp.einsum('jrd,jrc->jdc', inputs, gathered, preferred_element_type=jnp.f...]
    all_to_all x1 -> x0, local copies, waits for them, and re-layouts: 40.6 us -> none  [per_device(): lax.all_to_all(stacked, 'section', split_axis=3, concat_axis=0, tiled=True)]
    broadcast_in_dim x1 -> x0, local copies, waits for them, and re-layouts: 23.9 us -> none  [per_device(): stacked = jnp.stack(blocks)[None]]
  transfers between devices with their start and end apart: 2 -> 0, of which waited for: 2 -> 0; matrix products, arithmetic and copies ran while one was open for 0% -> 0% of each run, Pallas kernels for 0% -> 0%
where the time goes in v1:
time: 326 us; the launch traced here: 325 us
  Pallas kernels  290 us (89%)
  other arithmetic  19.1 us (6%)
  local copies, waits for them, and re-layouts  13.1 us (4%)
    pallas_call x1, Pallas kernels, per_device(): pl.pallas_call(gather_multiply, name='gather_multiply', out_shape=(blocks...  181 us
    pallas_call x1, Pallas kernels, per_device(): pl.pallas_call(merge, name='merge', out_shape=jax.ShapeDtypeStruct((LAYER...  110 us
    unnamed x3, local copies, waits for them, and re-layouts  7.59 us
    select_n x6, other arithmetic, tables(): slots.append(jnp.where(live, 2 * slot + q % 2 + UNITS * (q // 2), 0))  7.47 us
    and x6, other arithmetic, tables(): live = (slot >= 0) & (layers < high[section])  7.47 us

profile of v1, /device:TPU:0, one launch (start us, length us, event | category | flops | bytes accessed | tf_op | source)
XLA Modules:
  0.0 325.4 jit_solution(15149027099478872774)
XLA Ops:
  0.0 0.0 copy-start
  0.0 0.7 fusion
  0.7 0.6 dynamic_slice.58
  3.2 1.2 dynamic_slice.59
  5.1 0.0 copy-done
  5.1 0.7 gather_fusion
  5.8 0.7 gather_fusion.1
  6.5 0.7 fusion.8
  7.2 1.2 add_select_fusion
  8.4 1.2 compare_and_fusion
  9.7 1.2 add_select_fusion.1
  10.9 1.2 compare_and_fusion.1
  12.2 1.2 add_select_fusion.2
  13.4 1.2 compare_and_fusion.2
  14.7 1.2 add_select_fusion.3
  15.9 1.2 compare_and_fusion.3
  17.1 1.3 add_select_fusion.4
  18.4 1.3 compare_and_fusion.4
  19.7 1.2 multiply_select_fusion
  21.0 1.2 compare_and_fusion.5
  22.3 0.1 copy.9
  22.4 0.7 reshape.216.weight_of
  23.1 0.1 copy.8
  23.2 0.7 reshape.211.slot_of
  23.9 3.5 %bitcast_select_fusion.c_ref = bf16[5,1024,256]{2,1,0:T(8,128)(2,1)} fusion(bf16[1,5,1024,256]{3,2,1,0:T(8,128)(2,1)} %param.6, pred[1024]{0:T(1024)(128)(4,1)S(1)} %iota_compare_fusion), kind=kLoop, calls=%fused_computation.2 | loop fusion | flops 1310720 | bytes 5243904 | tf_op jit(solution)/shard_map/jit(_where)/select_n | solution.py:367
  27.3 180.5 %gather_multiply.1 = (bf16[10,2,512,512]{3,2,1,0:T(8,128)(2,1)}, bf16[10,2,512,512]{3,2,1,0:T(8,128)(2,1)}, bf16[5,1024,1024]{2,1,0:T(8,128)(2,1)}) custom-call(bf16[5,1024,256]{2,1,0:T(8,128)(2,1)} %bitcast_select_fusion.c_ref, bf16[5,1024,1024]{2,1,0:T(8,128)(2,1)} %bitcast.23), custom_call_target="tpu_custom_call" | custom-call | tf_op jit(solution)/shard_map/gather_multiply/pallas_call | solution.py:372
  207.9 109.9 %merge.1 = f32[16,1024,128]{2,1,0:T(8,128)} custom-call(s32[128]{0:T(128)} %reshape.211.slot_of, f32[128]{0:T(128)} %reshape.216.weight_of, bf16[10,2,512,512]{3,2,1,0:T(8,128)(2,1)} %get-tuple-element.7.kept, bf16[10,2,512,512]{3,2,1,0:T(8,128)(2,1)} %get-tuple-element.8.recv), custom_call_target="tpu_custom_call" | custom-call | tf_op jit(solution)/shard_map/merge/pallas_call | solution.py:390
  317.8 7.6 %copy.11 = f32[16,1024,128]{2,1,0:T(8,128)} copy(f32[16,1024,128]{2,1,0:T(8,128)} %merge.1) | data formatting | bytes 16777216
  (4 shorter events, 0.1 us)
Async XLA Ops:
  0.0 5.1 %copy-start = (s32[3,17]{1,0:T(4,128)S(1)}, s32[3,17]{1,0:T(4,128)}, u32[]{:S(2)}) copy-start(s32[3,17]{1,0:T(4,128)} %param.8) | copy-start | bytes 616

commit v2 on v1

--- a/solution.py
+++ b/solution.py
@@ -36,7 +36,7 @@
 
 
 def gather_multiply(
-    c_ref, a_ref, kept, recv, a2, cbuf, abuf, stk, sts,
+    code, micro, c_ref, a_ref, kept, recv, a2, cbuf, abuf, stk, sts,
     loc_sem, cs_sem, cr_sem, as_sem, ar_sem, ms_sem, mr_sem, al_sem, k_sem, ps_sem, pr_sem,
 ):
     yh, x, c, yl, z = place()
@@ -76,6 +76,10 @@
         )
 
     half = ROWS // 2
+    own_section = (yh * 4 + x) * 2 + c
+    limits = [
+        MBT * micro[section_part(code, section)[0]] for section in (own_section, own_section + 1 - 2 * c)
+    ]
 
     def message(kind, s):
         if kind <= 2:
@@ -166,6 +170,10 @@
             def _():
                 mate_c(it // 2).wait_recv()
 
+            own_column = pl.ds(column(yl, z), 128)
+            limit = jnp.where(it % 2 == 0, limits[0], limits[1])
+            live = (lax.broadcasted_iota(jnp.int32, (ROWS, 128), 0) < limit).astype(jnp.float32)
+            cbuf[it, :, own_column] = (cbuf[it, :, own_column].astype(jnp.float32) * live).astype(jnp.bfloat16)
             for kind in (0, 1, 2):
                 message(kind, it).start()
 
@@ -220,15 +228,15 @@
 
 
 def merge(
-    slot_of, weight_of, kept, recv, out, ld_even, ld_odd, p2k, p2s, p2r, p3k, p3s, p3r, ost,
+    code, bounds, kept, recv, own_sum, peer_sum, ld_even, ld_odd, p2k, p2s, p2r, p3k, p3s, slot_of, weight_of,
     ld_sem, s2_sem, r2_sem, s3_sem, r3_sem, o_sem,
 ):
     yh, x, c, yl, z = place()
-    peer_a = device(yh, x + 1 - 2 * (x % 2), c, yl, z)
-    peer_b = device(yh, 3 - x, c, yl, z)
+    xa = x + 1 - 2 * (x % 2)
+    xb = 3 - x
+    peer_a = device(yh, xa, c, yl, z)
+    peer_b = device(yh, xb, c, yl, z)
     peer_y = device(1 - yh, x, c, yl, z)
-    greet((peer_a, peer_b, peer_y))
-
     ld = (ld_even, ld_odd)
 
     def loads(n, b):
@@ -245,18 +253,35 @@
             device_id=(peer_b, peer_a)[h], device_id_type=MESH,
         )
 
-    def send_y(n, b):
-        return pltpu.make_async_remote_copy(
-            p3s.at[b], p3r.at[n], s3_sem.at[b], r3_sem.at[n], device_id=peer_y, device_id_type=MESH
+    def send_y(n, b, h):
+        rows = pl.ds(pl.multiple_of(h * 512 + n * CROWS, CROWS), CROWS)
+        return pltpu.make_async_remote_copy(
+            p3s.at[b, h], peer_sum.at[:, rows, :], s3_sem.at[b, h], r3_sem.at[n, h],
+            device_id=peer_y, device_id_type=MESH,
         )
 
     def store(n, b, h):
         return pltpu.make_async_copy(
-            ost.at[b, h], out.at[:, pl.ds(pl.multiple_of(h * 512 + n * CROWS, CROWS), CROWS), :], o_sem.at[b, h]
+            p3k.at[b, h], own_sum.at[:, pl.ds(pl.multiple_of(h * 512 + n * CROWS, CROWS), CROWS), :], o_sem.at[b, h]
         )
 
     for load in loads(0, 0):
         load.start()
+    for h, partner in enumerate((xa, xb)):
+        sections = ((x, c), (x, 1 - c), (partner, c), (partner, 1 - c))
+        for q, (sx, sc) in enumerate(sections):
+            replica, part = section_part(code, (yh * 4 + sx) * 2 + sc)
+            low = bounds[replica, part]
+            high = bounds[replica, part + 1]
+
+            @pl.loop(0, LAYERS)
+            def _(layer):
+                live = (layer >= low) & (layer < high)
+                at = (h * LAYERS + layer) * 4 + q
+                slot_of[at] = jnp.where(live, 2 * (layer - low) + (q % 2) + UNITS * (q // 2), 0)
+                weight_of[at] = jnp.where(live, 1.0, 0.0)
+
+    greet((peer_a, peer_b, peer_y))
 
     def first(n, b):
         @pl.when(n + 1 < CHUNKS)
@@ -286,7 +311,9 @@
     def second(n, b):
         @pl.when(n >= 2)
         def _():
-            send_y(n - 2, b).wait_send()
+            for h in range(2):
+                send_y(n - 2, b, h).wait_send()
+                store(n - 2, b, h).wait()
 
         for h in range(2):
             send_x(n, b, h).wait_recv()
@@ -297,19 +324,7 @@
                 p3k[b, h, layer] = total[:, 0:128]
                 p3s[b, h, layer] = total[:, 128:256].astype(jnp.bfloat16)
 
-        send_y(n, b).start()
-
-    def third(n, b):
-        send_y(n, b).wait_recv()
-        for h in range(2):
-            @pl.when(n >= 2)
-            def _():
-                store(n - 2, b, h).wait()
-
-            @pl.loop(0, LAYERS)
-            def _(layer):
-                ost[b, h, layer] = p3k[b, h, layer] + p3r[n, h, layer].astype(jnp.float32)
-
+            send_y(n, b, h).start()
             store(n, b, h).start()
 
     @pl.loop(0, CHUNKS // 2 + 1)
@@ -325,46 +340,27 @@
             def _():
                 second(n - 1, 1 - b)
 
-            @pl.when(n >= 2)
-            def _():
-                third(n - 2, b)
-
     for b in range(2):
         n = CHUNKS - 2 + b
-        send_y(n, b).wait_send()
         for h in range(2):
             send_x(n, b, h).wait_send()
+            send_y(n, b, h).wait_send()
             store(n, b, h).wait()
 
-
-def tables(section_code, boundaries):
-    replica = (section_code >= 4).astype(jnp.int32) + (section_code >= 9).astype(jnp.int32)
-    part = section_code - jnp.where(replica == 0, 0, jnp.where(replica == 1, 4, 9))
-    low = boundaries[replica, part]
-    high = boundaries[replica, part + 1]
-    own = lax.axis_index("section")
-    x = (own // 2) % 4
-    base = own - 2 * x
-    mate = own + 1 - 2 * (own % 2)
-    slots, weights = [], []
-    layers = jnp.arange(LAYERS, dtype=jnp.int32)
-    for partner_x in (x + 1 - 2 * (x % 2), 3 - x):
-        partner = base + 2 * partner_x
-        partner_mate = partner + 1 - 2 * (partner % 2)
-        for q, section in enumerate((own, mate, partner, partner_mate)):
-            slot = layers - low[section]
-            live = (slot >= 0) & (layers < high[section])
-            slots.append(jnp.where(live, 2 * slot + (q % 2) + UNITS * (q // 2), 0))
-            weights.append(live.astype(jnp.float32))
-    order = lambda v: jnp.stack(v).reshape(2, 4, LAYERS).transpose(0, 2, 1).reshape(-1)
-    return replica, order(slots).astype(jnp.int32), order(weights)
+    @pl.loop(0, CHUNKS)
+    def _(n):
+        for h in range(2):
+            send_y(n, 0, h).wait_recv()
+
+
+def section_part(code, section):
+    value = code[section]
+    second = jnp.where(value >= 4, 1, 0)
+    third = jnp.where(value >= 9, 1, 0)
+    return second + third, value - 4 * second - 5 * third
 
 
 def per_device(activations, cotangents, section_code, boundaries, micro_counts):
-    replica, slot_of, weight_of = tables(section_code, boundaries)
-    row_limit = MBT * micro_counts[replica[lax.axis_index("section")]]
-    live_rows = (jnp.arange(ROWS, dtype=jnp.int32) < row_limit)[None, :, None]
-    masked = jnp.where(live_rows, cotangents[0], jnp.zeros((), jnp.bfloat16))
     any_spec = pl.BlockSpec(memory_space=pl.ANY)
     smem_spec = pl.BlockSpec(memory_space=pltpu.SMEM)
     dma = pltpu.SemaphoreType.DMA
@@ -373,7 +369,7 @@
         gather_multiply,
         name="gather_multiply",
         out_shape=(blocks, blocks, jax.ShapeDtypeStruct((SLOTS, ROWS, WIDTH), jnp.bfloat16)),
-        in_specs=[any_spec] * 2,
+        in_specs=[smem_spec] * 2 + [any_spec] * 2,
         out_specs=(any_spec,) * 3,
         scratch_shapes=[
             pltpu.VMEM((UNITS, ROWS, 1024), jnp.bfloat16),
@@ -386,13 +382,16 @@
         compiler_params=pltpu.CompilerParams(
             collective_id=0, has_side_effects=True, vmem_limit_bytes=56 << 20
         ),
-    )(masked, activations[0])
-    return pl.pallas_call(
+    )(section_code, micro_counts, cotangents[0], activations[0])
+    own_sum, peer_sum = pl.pallas_call(
         merge,
         name="merge",
-        out_shape=jax.ShapeDtypeStruct((LAYERS, WIDTH, 128), jnp.float32),
+        out_shape=(
+            jax.ShapeDtypeStruct((LAYERS, WIDTH, 128), jnp.float32),
+            jax.ShapeDtypeStruct((LAYERS, WIDTH, 128), jnp.bfloat16),
+        ),
         in_specs=[smem_spec, smem_spec, any_spec, any_spec],
-        out_specs=any_spec,
+        out_specs=(any_spec, any_spec),
         scratch_shapes=[
             pltpu.VMEM((2, 2 * UNITS, CROWS, 512), jnp.bfloat16),
             pltpu.VMEM((2, 2 * UNITS, CROWS, 512), jnp.bfloat16),
@@ -401,14 +400,15 @@
             pltpu.VMEM((CHUNKS, 2, LAYERS, CROWS, 256), jnp.bfloat16),
             pltpu.VMEM((2, 2, LAYERS, CROWS, 128), jnp.float32),
             pltpu.VMEM((2, 2, LAYERS, CROWS, 128), jnp.bfloat16),
-            pltpu.VMEM((CHUNKS, 2, LAYERS, CROWS, 128), jnp.bfloat16),
-            pltpu.VMEM((2, 2, LAYERS, CROWS, 128), jnp.float32),
-            dma((2, 2, 2)), dma((2, 2)), dma((CHUNKS, 2)), dma((2,)), dma((CHUNKS,)), dma((2, 2)),
+            pltpu.SMEM((2 * LAYERS * 4,), jnp.int32),
+            pltpu.SMEM((2 * LAYERS * 4,), jnp.float32),
+            dma((2, 2, 2)), dma((2, 2)), dma((CHUNKS, 2)), dma((2, 2)), dma((CHUNKS, 2)), dma((2, 2)),
         ],
         compiler_params=pltpu.CompilerParams(
             collective_id=1, has_side_effects=True, vmem_limit_bytes=56 << 20
         ),
-    )(slot_of, weight_of, kept, recv)
+    )(section_code, boundaries, kept, recv)
+    return own_sum + peer_sum.astype(jnp.float32)
 
 
 def solution(mesh):

time: 326 us -> 299 us (0.917)
  local copies, waits for them, and re-layouts: 13.1 us -> 0 us
  other arithmetic: 19.1 us -> 8.8 us
    select_n x7 -> x0, other arithmetic: 11 us -> none  [the longest x6 7.47 us: tables(): slots.append(jnp.where(live, 2 * slot + q % 2 + UNITS * (q // 2), 0))]
    add x1, other arithmetic: 0.68 us -> 8.8 us  [per_device(): return own_sum + peer_sum.astype(jnp.float32)]
    unnamed x3 -> x0, local copies, waits for them, and re-layouts: 7.59 us -> none
    and x6 -> x0, other arithmetic: 7.47 us -> none  [tables(): live = (slot >= 0) & (layers < high[section])]
where the time goes in v2:
time: 299 us
  Pallas kernels  290 us (97%)
  other arithmetic  8.8 us (3%)
    pallas_call x1, Pallas kernels, per_device(): pl.pallas_call(gather_multiply, name='gather_multiply', out_shape=(blocks...  181 us
    pallas_call x1, Pallas kernels, per_device(): pl.pallas_call(merge, name='merge', out_shape=(jax.ShapeDtypeStruct((LAYE...  108 us
    add x1, other arithmetic, per_device(): return own_sum + peer_sum.astype(jnp.float32)  8.8 us

profile of v2, /device:TPU:0, one launch (start us, length us, event | category | flops | bytes accessed | tf_op | source)
XLA Modules:
  0.0 298.5 jit_solution(9216480800989568465)
XLA Ops:
  0.0 181.3 %gather_multiply.1 = (bf16[10,2,512,512]{3,2,1,0:T(8,128)(2,1)}, bf16[10,2,512,512]{3,2,1,0:T(8,128)(2,1)}, bf16[5,1024,1024]{2,1,0:T(8,128)(2,1)}) custom-call(s32[16]{0:T(128)} %code.3, s32[3]{0:T(128)} %micro.1, bf16[5,1024,256]{2,1,0:T(8,128)(2,1)} %bitcast.3, bf16[5,1024,1024]{2,1,0:T(8,128)(2,1)} %bitcast.2), custom_call_target="tpu_custom_call" | custom-call | tf_op jit(solution)/shard_map/gather_multiply/pallas_call | solution.py:368
  181.4 108.4 %merge.1 = (f32[16,1024,128]{2,1,0:T(8,128)}, bf16[16,1024,128]{2,1,0:T(8,128)(2,1)}) custom-call(s32[16]{0:T(128)} %code.3, s32[3,17]{1,0:T(4,128)} %bounds.1, bf16[10,2,512,512]{3,2,1,0:T(8,128)(2,1)} %get-tuple-element.9.kept, bf16[10,2,512,512]{3,2,1,0:T(8,128)(2,1)} %get-tuple-element.10.recv), custom_call_target="tpu_custom_call" | custom-call | tf_op jit(solution)/shard_map/merge/pallas_call | solution.py:386
  289.7 8.8 %convert_add_fusion = f32[16,1024,128]{2,1,0:T(8,128)} fusion(f32[16,1024,128]{2,1,0:T(8,128)} %get-tuple-element.11, bf16[16,1024,128]{2,1,0:T(8,128)(2,1)} %get-tuple-element.12), kind=kLoop, calls=%fused_computation | loop fusion | flops 4194304 | bytes 20971520 | tf_op jit(solution)/shard_map/add | solution.py:411

commit v3 on v2

--- a/solution.py
+++ b/solution.py
@@ -14,7 +14,8 @@
 ROWS = 1024
 WIDTH = 1024
 LAYERS = 16
-CHUNKS = 8
+CHUNKS = 16
+SPLIT = 176
 CROWS = 512 // CHUNKS
 
 
@@ -35,9 +36,11 @@
     pl.semaphore_wait(barrier, len(peers))
 
 
-def gather_multiply(
-    code, micro, c_ref, a_ref, kept, recv, a2, cbuf, abuf, stk, sts,
+def gradients(
+    code, bounds, micro, c_ref, a_ref, own_sum, peer_sum, kept, recv, a2,
+    cbuf, abuf, stk, sts, ld_even, ld_odd, p2k, p2s, p2r, p3k, p3s, slot_of, weight_of,
     loc_sem, cs_sem, cr_sem, as_sem, ar_sem, ms_sem, mr_sem, al_sem, k_sem, ps_sem, pr_sem,
+    ld_sem, s2_sem, r2_sem, s3_sem, r3_sem, o_sem,
 ):
     yh, x, c, yl, z = place()
     xa = x + 1 - 2 * (x % 2)
@@ -48,7 +51,9 @@
     zminus = device(yh, x, c, yl, (z + 3) % 4)
     peer_a = device(yh, xa, c, yl, z)
     peer_b = device(yh, xb, c, yl, z)
-    greet((mate, ypeer, zplus, zminus, peer_a, peer_b))
+    peer_y = device(1 - yh, x, c, yl, z)
+    ld = (ld_even, ld_odd)
+    greet((mate, ypeer, zplus, zminus, peer_a, peer_b, peer_y))
     turn = 1 + 2 * (x % 2)
 
     def column(yy, zz):
@@ -85,13 +90,15 @@
         if kind <= 2:
             ref, target = shard(s, yl, z), (ypeer, zplus, zminus)[kind]
         elif kind <= 4:
-            ref, target = shard(s, 1 - yl, z), (zplus, zminus)[kind - 3]
+            ref, target = shard(s, 1 - yl, z, SPLIT, ROWS - SPLIT), (zplus, zminus)[kind - 3]
         elif kind == 5:
             ref, target = shard(s, yl, z + 3, 0, half), zplus
         elif kind == 6:
             ref, target = shard(s, yl, z + 1, half, half), zminus
+        elif kind == 7:
+            ref, target = shard(s, yl, z + 2), ypeer
         else:
-            ref, target = shard(s, yl, z + 2), ypeer
+            ref, target = shard(s, yl, (z + 3, z + 1)[kind - 8], 0, SPLIT), ypeer
         return pltpu.make_async_remote_copy(
             ref, ref, ms_sem.at[kind, s], mr_sem.at[kind, s], device_id=target, device_id_type=MESH
         )
@@ -105,9 +112,10 @@
     def keep(s, b):
         return pltpu.make_async_copy(stk.at[b], kept.at[s], k_sem.at[b])
 
-    def swap(s, b, h):
-        return pltpu.make_async_remote_copy(
-            sts.at[b, h], recv.at[s, h], ps_sem.at[b, h], pr_sem.at[s, h],
+    def swap(s, b, h, tile):
+        rows = pl.ds(pl.multiple_of(tile * 256, 256), 256)
+        return pltpu.make_async_remote_copy(
+            sts.at[b, h, rows], recv.at[s, h, rows], ps_sem.at[b, h, tile], pr_sem.at[s, h, tile],
             device_id=(peer_a, peer_b)[h], device_id_type=MESH,
         )
 
@@ -134,18 +142,19 @@
         @pl.when(j > 0)
         def _():
             keep(s - 2, b).wait()
-            swap(s - 2, b, 0).wait_send()
-            swap(s - 2, b, 1).wait_send()
-
-        for h in range(2):
-            @pl.loop(0, 2)
-            def _(tile):
-                at = pl.multiple_of(tile * 256, 256)
+            for h in range(2):
+                for tile in range(2):
+                    swap(s - 2, b, h, tile).wait_send()
+
+        @pl.loop(0, 2)
+        def _(tile):
+            at = pl.multiple_of(tile * 256, 256)
+            rows = pl.ds(at, 256)
+            for h in range(2):
                 block = lax.dot_general(
                     abuf[b, :, pl.ds(h * 512 + at, 256)], cbuf[s],
                     (((0,), (0,)), ((), ())), preferred_element_type=jnp.float32,
                 ).astype(jnp.bfloat16)
-                rows = pl.ds(at, 256)
                 if h == 0:
                     sts[b, 0, rows, :] = block[:, 256:768]
                     stk[b, 0, rows, 0:256] = block[:, 0:256]
@@ -154,8 +163,8 @@
                     sts[b, 1, rows, 0:256] = block[:, 768:1024]
                     sts[b, 1, rows, 256:512] = block[:, 512:768]
                     stk[b, 1, rows, :] = block[:, 0:512]
-
-            swap(s, b, h).start()
+                swap(s, b, h, tile).start()
+
         keep(s, b).start()
 
     @pl.loop(0, UNITS + 3)
@@ -185,8 +194,10 @@
             message(4, s).start()
             message(1, s).wait_recv()
             message(5, s).start()
+            message(8, s).start()
             message(2, s).wait_recv()
             message(6, s).start()
+            message(9, s).start()
 
         @pl.when((it >= 2) & (it < UNITS + 2))
         def _():
@@ -200,7 +211,8 @@
             s = it - 3
             message(3, s).wait_recv()
             message(4, s).wait_recv()
-            message(7, s).wait_recv()
+            for kind in (7, 8, 9):
+                message(kind, s).wait_recv()
 
             @pl.when(s % 2 == 0)
             def _():
@@ -210,34 +222,28 @@
             def _():
                 compute(s, 1)
 
+    for h, partner in enumerate((xa, xb)):
+        sections = ((x, c), (x, 1 - c), (partner, c), (partner, 1 - c))
+        for q, (sx, sc) in enumerate(sections):
+            replica, part = section_part(code, (yh * 4 + sx) * 2 + sc)
+            low = bounds[replica, part]
+            high = bounds[replica, part + 1]
+
+            @pl.loop(0, LAYERS)
+            def _(layer):
+                live = (layer >= low) & (layer < high)
+                at = (h * LAYERS + layer) * 4 + q
+                slot_of[at] = jnp.where(live, 2 * (layer - low) + (q % 2) + UNITS * (q // 2), 0)
+                weight_of[at] = jnp.where(live, 1.0, 0.0)
+
     for b in range(2):
-        s = UNITS - 2 + b
-        keep(s, b).wait()
-        swap(s, b, 0).wait_send()
-        swap(s, b, 1).wait_send()
-    for j in range(SLOTS):
-        mate_c(j).wait_send()
-        mate_a(j).wait_send()
-
-    @pl.loop(0, UNITS)
-    def _(s):
-        for kind in range(8):
-            message(kind, s).wait_send()
-        for h in range(2):
-            swap(s, 0, h).wait_recv()
-
-
-def merge(
-    code, bounds, kept, recv, own_sum, peer_sum, ld_even, ld_odd, p2k, p2s, p2r, p3k, p3s, slot_of, weight_of,
-    ld_sem, s2_sem, r2_sem, s3_sem, r3_sem, o_sem,
-):
-    yh, x, c, yl, z = place()
-    xa = x + 1 - 2 * (x % 2)
-    xb = 3 - x
-    peer_a = device(yh, xa, c, yl, z)
-    peer_b = device(yh, xb, c, yl, z)
-    peer_y = device(1 - yh, x, c, yl, z)
-    ld = (ld_even, ld_odd)
+        keep(UNITS - 2 + b, b).wait()
+
+    def arrived(tile):
+        @pl.loop(0, UNITS)
+        def _(s):
+            for h in range(2):
+                swap(s, 0, h, tile).wait_recv()
 
     def loads(n, b):
         rows = pl.ds(pl.multiple_of(n * CROWS, CROWS), CROWS)
@@ -265,25 +271,19 @@
             p3k.at[b, h], own_sum.at[:, pl.ds(pl.multiple_of(h * 512 + n * CROWS, CROWS), CROWS), :], o_sem.at[b, h]
         )
 
-    for load in loads(0, 0):
-        load.start()
-    for h, partner in enumerate((xa, xb)):
-        sections = ((x, c), (x, 1 - c), (partner, c), (partner, 1 - c))
-        for q, (sx, sc) in enumerate(sections):
-            replica, part = section_part(code, (yh * 4 + sx) * 2 + sc)
-            low = bounds[replica, part]
-            high = bounds[replica, part + 1]
-
-            @pl.loop(0, LAYERS)
-            def _(layer):
-                live = (layer >= low) & (layer < high)
-                at = (h * LAYERS + layer) * 4 + q
-                slot_of[at] = jnp.where(live, 2 * (layer - low) + (q % 2) + UNITS * (q // 2), 0)
-                weight_of[at] = jnp.where(live, 1.0, 0.0)
-
-    greet((peer_a, peer_b, peer_y))
-
     def first(n, b):
+        if b == 0:
+            @pl.when(n == 0)
+            def _():
+                arrived(0)
+                for load in loads(0, 0):
+                    load.start()
+
+        else:
+            @pl.when(n == CHUNKS // 2 - 1)
+            def _():
+                arrived(1)
+
         @pl.when(n + 1 < CHUNKS)
         def _():
             for load in loads(n + 1, 1 - b):
@@ -347,6 +347,19 @@
             send_y(n, b, h).wait_send()
             store(n, b, h).wait()
 
+    for b in range(2):
+        for h in range(2):
+            for tile in range(2):
+                swap(UNITS - 2 + b, b, h, tile).wait_send()
+    for j in range(SLOTS):
+        mate_c(j).wait_send()
+        mate_a(j).wait_send()
+
+    @pl.loop(0, UNITS)
+    def _(s):
+        for kind in range(10):
+            message(kind, s).wait_send()
+
     @pl.loop(0, CHUNKS)
     def _(n):
         for h in range(2):
@@ -365,34 +378,23 @@
     smem_spec = pl.BlockSpec(memory_space=pltpu.SMEM)
     dma = pltpu.SemaphoreType.DMA
     blocks = jax.ShapeDtypeStruct((UNITS, 2, 512, 512), jnp.bfloat16)
-    kept, recv, _ = pl.pallas_call(
-        gather_multiply,
-        name="gather_multiply",
-        out_shape=(blocks, blocks, jax.ShapeDtypeStruct((SLOTS, ROWS, WIDTH), jnp.bfloat16)),
-        in_specs=[smem_spec] * 2 + [any_spec] * 2,
-        out_specs=(any_spec,) * 3,
+    own_sum, peer_sum, _, _, _ = pl.pallas_call(
+        gradients,
+        name="gradients",
+        out_shape=(
+            jax.ShapeDtypeStruct((LAYERS, WIDTH, 128), jnp.float32),
+            jax.ShapeDtypeStruct((LAYERS, WIDTH, 128), jnp.bfloat16),
+            blocks,
+            blocks,
+            jax.ShapeDtypeStruct((SLOTS, ROWS, WIDTH), jnp.bfloat16),
+        ),
+        in_specs=[smem_spec] * 3 + [any_spec] * 2,
+        out_specs=(any_spec,) * 5,
         scratch_shapes=[
             pltpu.VMEM((UNITS, ROWS, 1024), jnp.bfloat16),
             pltpu.VMEM((2, ROWS, WIDTH), jnp.bfloat16),
             pltpu.VMEM((2, 2, 512, 512), jnp.bfloat16),
             pltpu.VMEM((2, 2, 512, 512), jnp.bfloat16),
-            dma((SLOTS,)), dma((SLOTS,)), dma((SLOTS,)), dma((SLOTS,)), dma((SLOTS,)),
-            dma((8, UNITS)), dma((8, UNITS)), dma((2,)), dma((2,)), dma((2, 2)), dma((UNITS, 2)),
-        ],
-        compiler_params=pltpu.CompilerParams(
-            collective_id=0, has_side_effects=True, vmem_limit_bytes=56 << 20
-        ),
-    )(section_code, micro_counts, cotangents[0], activations[0])
-    own_sum, peer_sum = pl.pallas_call(
-        merge,
-        name="merge",
-        out_shape=(
-            jax.ShapeDtypeStruct((LAYERS, WIDTH, 128), jnp.float32),
-            jax.ShapeDtypeStruct((LAYERS, WIDTH, 128), jnp.bfloat16),
-        ),
-        in_specs=[smem_spec, smem_spec, any_spec, any_spec],
-        out_specs=(any_spec, any_spec),
-        scratch_shapes=[
             pltpu.VMEM((2, 2 * UNITS, CROWS, 512), jnp.bfloat16),
             pltpu.VMEM((2, 2 * UNITS, CROWS, 512), jnp.bfloat16),
             pltpu.VMEM((2, 2, LAYERS, CROWS, 256), jnp.float32),
@@ -402,12 +404,14 @@
             pltpu.VMEM((2, 2, LAYERS, CROWS, 128), jnp.bfloat16),
             pltpu.SMEM((2 * LAYERS * 4,), jnp.int32),
             pltpu.SMEM((2 * LAYERS * 4,), jnp.float32),
+            dma((SLOTS,)), dma((SLOTS,)), dma((SLOTS,)), dma((SLOTS,)), dma((SLOTS,)),
+            dma((10, UNITS)), dma((10, UNITS)), dma((2,)), dma((2,)), dma((2, 2, 2)), dma((UNITS, 2, 2)),
             dma((2, 2, 2)), dma((2, 2)), dma((CHUNKS, 2)), dma((2, 2)), dma((CHUNKS, 2)), dma((2, 2)),
         ],
         compiler_params=pltpu.CompilerParams(
-            collective_id=1, has_side_effects=True, vmem_limit_bytes=56 << 20
+            collective_id=0, has_side_effects=True, vmem_limit_bytes=60 << 20
         ),
-    )(section_code, boundaries, kept, recv)
+    )(section_code, boundaries, micro_counts, cotangents[0], activations[0])
     return own_sum + peer_sum.astype(jnp.float32)
 
 

time: 299 us -> 281 us (0.940)
  Pallas kernels: 290 us -> 272 us
    pallas_call x2 -> x1, Pallas kernels: 290 us -> 272 us  [per_device(): pl.pallas_call(gradients, name='gradients', out_shape=(jax.ShapeDtypeStru...]
where the time goes in v3:
time: 281 us
  Pallas kernels  272 us (97%)
  other arithmetic  8.8 us (3%)
    pallas_call x1, Pallas kernels, per_device(): pl.pallas_call(gradients, name='gradients', out_shape=(jax.ShapeDtypeStru...  272 us
    add x1, other arithmetic, per_device(): return own_sum + peer_sum.astype(jnp.float32)  8.8 us

profile of v3, /device:TPU:0, one launch (start us, length us, event | category | flops | bytes accessed | tf_op | source)
XLA Modules:
  0.0 280.8 jit_solution(1306051123104210279)
XLA Ops:
  0.0 271.9 %gradients.1 = (f32[16,1024,128]{2,1,0:T(8,128)}, bf16[16,1024,128]{2,1,0:T(8,128)(2,1)}, bf16[10,2,512,512]{3,2,1,0:T(8,128)(2,1)}, bf16[10,2,512,512]{3,2,1,0:T(8,128)(2,1)}, bf16[5,1024,1024]{2,1,0:T(8,128)(2,1)}) custom-call(s32[16]{0:T(128)} %code.1, s32[3,17]{1,0:T(4,128)} %bounds.1, s32[3]{0:T(128)} %micro.1, bf16[5,1024,256]{2,1,0:T(8,128)(2,1)} %bitcast.3, ...), custom_call_target="tpu_custom_call" | custom-call | tf_op jit(solution)/shard_map/gradients/pallas_call | solution.py:381
  272.0 8.8 %convert_add_fusion = f32[16,1024,128]{2,1,0:T(8,128)} fusion(f32[16,1024,128]{2,1,0:T(8,128)} %get-tuple-element.7, bf16[16,1024,128]{2,1,0:T(8,128)(2,1)} %get-tuple-element.8), kind=kLoop, calls=%fused_computation | loop fusion | flops 4194304 | bytes 20971520 | tf_op jit(solution)/shard_map/add | solution.py:415

commit v4 on v3

--- a/solution.py
+++ b/solution.py
@@ -16,6 +16,9 @@
 LAYERS = 16
 CHUNKS = 16
 SPLIT = 176
+EARLY = 3
+LATE = LAYERS - EARLY
+EROWS = 64
 CROWS = 512 // CHUNKS
 
 
@@ -39,8 +42,10 @@
 def gradients(
     code, bounds, micro, c_ref, a_ref, own_sum, peer_sum, kept, recv, a2,
     cbuf, abuf, stk, sts, ld_even, ld_odd, p2k, p2s, p2r, p3k, p3s, slot_of, weight_of,
+    le_even, le_odd, q2k, q2s, q2r, q3k, q3s,
     loc_sem, cs_sem, cr_sem, as_sem, ar_sem, ms_sem, mr_sem, al_sem, k_sem, ps_sem, pr_sem,
     ld_sem, s2_sem, r2_sem, s3_sem, r3_sem, o_sem,
+    le_sem, t2_sem, u2_sem, t3_sem, u3_sem, v_sem,
 ):
     yh, x, c, yl, z = place()
     xa = x + 1 - 2 * (x % 2)
@@ -53,6 +58,7 @@
     peer_b = device(yh, xb, c, yl, z)
     peer_y = device(1 - yh, x, c, yl, z)
     ld = (ld_even, ld_odd)
+    le = (le_even, le_odd)
     greet((mate, ypeer, zplus, zminus, peer_a, peer_b, peer_y))
     turn = 1 + 2 * (x % 2)
 
@@ -167,7 +173,108 @@
 
         keep(s, b).start()
 
-    @pl.loop(0, UNITS + 3)
+    def tables():
+        for h, partner in enumerate((xa, xb)):
+            sections = ((x, c), (x, 1 - c), (partner, c), (partner, 1 - c))
+            for q, (sx, sc) in enumerate(sections):
+                replica, part = section_part(code, (yh * 4 + sx) * 2 + sc)
+                low = bounds[replica, part]
+                high = bounds[replica, part + 1]
+
+                @pl.loop(0, LAYERS)
+                def _(layer):
+                    live = (layer >= low) & (layer < high)
+                    at = (h * LAYERS + layer) * 4 + q
+                    slot_of[at] = jnp.where(live, 2 * (layer - low) + (q % 2), 0) + UNITS * (q // 2)
+                    weight_of[at] = jnp.where(live, 1.0, 0.0)
+
+    def early_loads(layer, block, b):
+        count = 2 * layer + 2
+        rows = pl.ds(pl.multiple_of(block * EROWS, EROWS), EROWS)
+        return [
+            pltpu.make_async_copy(
+                source.at[pl.ds(0, count), h, rows, :], le[b].at[h, pl.ds(g * count, count)], le_sem.at[b, h, g]
+            )
+            for h in range(2)
+            for g, source in enumerate((kept, recv))
+        ]
+
+    def early_x(layer, h):
+        b = layer % 2
+        return pltpu.make_async_remote_copy(
+            q2s.at[b, h], q2r.at[layer, h], t2_sem.at[b, h], u2_sem.at[layer, h],
+            device_id=(peer_b, peer_a)[h], device_id_type=MESH,
+        )
+
+    def early_y(layer, h):
+        b = layer % 2
+        return pltpu.make_async_remote_copy(
+            q3s.at[b, h], peer_sum.at[layer, pl.ds(h * 512, 512), :], t3_sem.at[b, h], u3_sem.at[layer, h],
+            device_id=peer_y, device_id_type=MESH,
+        )
+
+    def early_store(layer, h):
+        b = layer % 2
+        return pltpu.make_async_copy(q3k.at[b, h], own_sum.at[layer, pl.ds(h * 512, 512), :], v_sem.at[b, h])
+
+    def early_first(layer):
+        p = layer % 2
+        count = 2 * layer + 2
+        for s in (2 * layer, 2 * layer + 1):
+            for h in range(2):
+                for tile in range(2):
+                    swap(s, 0, h, tile).wait_recv()
+        if layer >= 2:
+            for h in range(2):
+                early_x(layer - 2, h).wait_send()
+        for load in early_loads(layer, 0, 0):
+            load.start()
+
+        @pl.loop(0, 512 // EROWS // 2)
+        def _(pair):
+            for b in range(2):
+                block = pair * 2 + b
+
+                @pl.when(block + 1 < 512 // EROWS)
+                def _():
+                    for load in early_loads(layer, block + 1, 1 - b):
+                        load.start()
+
+                for load in early_loads(layer, block, b):
+                    load.wait()
+                rows = pl.ds(pl.multiple_of(block * EROWS, EROWS), EROWS)
+                for h in range(2):
+                    total = None
+                    for q in range(4):
+                        at = (h * LAYERS + layer) * 4 + q
+                        slot = slot_of[at] + (q // 2) * (count - UNITS)
+                        term = le[b][h, slot].astype(jnp.float32) * weight_of[at]
+                        total = term if total is None else total + term
+                    q2k[p, h, rows, :] = total[:, 0:256]
+                    q2s[p, h, rows, :] = total[:, 256:512].astype(jnp.bfloat16)
+
+        for h in range(2):
+            early_x(layer, h).start()
+
+    def early_second(layer):
+        p = layer % 2
+        for h in range(2):
+            if layer >= 2:
+                early_y(layer - 2, h).wait_send()
+                early_store(layer - 2, h).wait()
+            early_x(layer, h).wait_recv()
+
+            @pl.loop(0, 512 // EROWS)
+            def _(block):
+                rows = pl.ds(pl.multiple_of(block * EROWS, EROWS), EROWS)
+                total = q2k[p, h, rows, :] + q2r[layer, h, rows, :].astype(jnp.float32)
+                q3k[p, h, rows, :] = total[:, 0:128]
+                q3s[p, h, rows, :] = total[:, 128:256].astype(jnp.bfloat16)
+
+            early_y(layer, h).start()
+            early_store(layer, h).start()
+
+    @pl.loop(0, UNITS + 1)
     def _(it):
         @pl.when(it < UNITS)
         def _():
@@ -186,32 +293,34 @@
             for kind in (0, 1, 2):
                 message(kind, it).start()
 
-        @pl.when((it >= 1) & (it < UNITS + 1))
+        @pl.when(it >= 1)
+        def _():
+            message(5, it - 1).wait_recv()
+            message(6, it - 1).wait_recv()
+            message(7, it - 1).start()
+
+        pl.when(it == 1)(tables)
+        for layer in range(EARLY):
+            pl.when(it == 2 * layer + 5)(functools.partial(early_first, layer))
+            if layer < EARLY - 1:
+                pl.when(it == 2 * layer + 7)(functools.partial(early_second, layer))
+
+        @pl.when(it < UNITS)
+        def _():
+            message(0, it).wait_recv()
+            message(3, it).start()
+            message(4, it).start()
+            message(1, it).wait_recv()
+            message(5, it).start()
+            message(8, it).start()
+            message(2, it).wait_recv()
+            message(6, it).start()
+            message(9, it).start()
+
+        @pl.when(it >= 1)
         def _():
             s = it - 1
-            message(0, s).wait_recv()
-            message(3, s).start()
-            message(4, s).start()
-            message(1, s).wait_recv()
-            message(5, s).start()
-            message(8, s).start()
-            message(2, s).wait_recv()
-            message(6, s).start()
-            message(9, s).start()
-
-        @pl.when((it >= 2) & (it < UNITS + 2))
-        def _():
-            s = it - 2
-            message(5, s).wait_recv()
-            message(6, s).wait_recv()
-            message(7, s).start()
-
-        @pl.when(it >= 3)
-        def _():
-            s = it - 3
-            message(3, s).wait_recv()
-            message(4, s).wait_recv()
-            for kind in (7, 8, 9):
+            for kind in (3, 4, 7, 8, 9):
                 message(kind, s).wait_recv()
 
             @pl.when(s % 2 == 0)
@@ -221,27 +330,12 @@
             @pl.when(s % 2 == 1)
             def _():
                 compute(s, 1)
-
-    for h, partner in enumerate((xa, xb)):
-        sections = ((x, c), (x, 1 - c), (partner, c), (partner, 1 - c))
-        for q, (sx, sc) in enumerate(sections):
-            replica, part = section_part(code, (yh * 4 + sx) * 2 + sc)
-            low = bounds[replica, part]
-            high = bounds[replica, part + 1]
-
-            @pl.loop(0, LAYERS)
-            def _(layer):
-                live = (layer >= low) & (layer < high)
-                at = (h * LAYERS + layer) * 4 + q
-                slot_of[at] = jnp.where(live, 2 * (layer - low) + (q % 2) + UNITS * (q // 2), 0)
-                weight_of[at] = jnp.where(live, 1.0, 0.0)
 
     for b in range(2):
         keep(UNITS - 2 + b, b).wait()
 
     def arrived(tile):
-        @pl.loop(0, UNITS)
-        def _(s):
+        for s in range(2 * EARLY, UNITS):
             for h in range(2):
                 swap(s, 0, h, tile).wait_recv()
 
@@ -262,13 +356,13 @@
     def send_y(n, b, h):
         rows = pl.ds(pl.multiple_of(h * 512 + n * CROWS, CROWS), CROWS)
         return pltpu.make_async_remote_copy(
-            p3s.at[b, h], peer_sum.at[:, rows, :], s3_sem.at[b, h], r3_sem.at[n, h],
+            p3s.at[b, h], peer_sum.at[pl.ds(EARLY, LATE), rows, :], s3_sem.at[b, h], r3_sem.at[n, h],
             device_id=peer_y, device_id_type=MESH,
         )
 
     def store(n, b, h):
         return pltpu.make_async_copy(
-            p3k.at[b, h], own_sum.at[:, pl.ds(pl.multiple_of(h * 512 + n * CROWS, CROWS), CROWS), :], o_sem.at[b, h]
+            p3k.at[b, h], own_sum.at[pl.ds(EARLY, LATE), pl.ds(pl.multiple_of(h * 512 + n * CROWS, CROWS), CROWS), :], o_sem.at[b, h]
         )
 
     def first(n, b):
@@ -296,11 +390,11 @@
             def _():
                 send_x(n - 2, b, h).wait_send()
 
-            @pl.loop(0, LAYERS)
+            @pl.loop(0, LATE)
             def _(layer):
                 total = None
                 for q in range(4):
-                    at = (h * LAYERS + layer) * 4 + q
+                    at = (h * LAYERS + EARLY + layer) * 4 + q
                     term = ld[b][h, slot_of[at]].astype(jnp.float32) * weight_of[at]
                     total = term if total is None else total + term
                 p2k[b, h, layer] = total[:, 0:256]
@@ -318,7 +412,7 @@
         for h in range(2):
             send_x(n, b, h).wait_recv()
 
-            @pl.loop(0, LAYERS)
+            @pl.loop(0, LATE)
             def _(layer):
                 total = p2k[b, h, layer] + p2r[n, h, layer].astype(jnp.float32)
                 p3k[b, h, layer] = total[:, 0:128]
@@ -329,6 +423,10 @@
 
     @pl.loop(0, CHUNKS // 2 + 1)
     def _(it):
+        @pl.when(it == 1)
+        def _():
+            early_second(EARLY - 1)
+
         for b in range(2):
             n = it * 2 + b
 
@@ -354,6 +452,14 @@
     for j in range(SLOTS):
         mate_c(j).wait_send()
         mate_a(j).wait_send()
+
+    for layer in range(EARLY):
+        for h in range(2):
+            early_y(layer, h).wait_recv()
+            if layer >= EARLY - 2:
+                early_x(layer, h).wait_send()
+                early_y(layer, h).wait_send()
+                early_store(layer, h).wait()
 
     @pl.loop(0, UNITS)
     def _(s):
@@ -397,16 +503,24 @@
             pltpu.VMEM((2, 2, 512, 512), jnp.bfloat16),
             pltpu.VMEM((2, 2 * UNITS, CROWS, 512), jnp.bfloat16),
             pltpu.VMEM((2, 2 * UNITS, CROWS, 512), jnp.bfloat16),
-            pltpu.VMEM((2, 2, LAYERS, CROWS, 256), jnp.float32),
-            pltpu.VMEM((2, 2, LAYERS, CROWS, 256), jnp.bfloat16),
-            pltpu.VMEM((CHUNKS, 2, LAYERS, CROWS, 256), jnp.bfloat16),
-            pltpu.VMEM((2, 2, LAYERS, CROWS, 128), jnp.float32),
-            pltpu.VMEM((2, 2, LAYERS, CROWS, 128), jnp.bfloat16),
+            pltpu.VMEM((2, 2, LATE, CROWS, 256), jnp.float32),
+            pltpu.VMEM((2, 2, LATE, CROWS, 256), jnp.bfloat16),
+            pltpu.VMEM((CHUNKS, 2, LATE, CROWS, 256), jnp.bfloat16),
+            pltpu.VMEM((2, 2, LATE, CROWS, 128), jnp.float32),
+            pltpu.VMEM((2, 2, LATE, CROWS, 128), jnp.bfloat16),
             pltpu.SMEM((2 * LAYERS * 4,), jnp.int32),
             pltpu.SMEM((2 * LAYERS * 4,), jnp.float32),
+            pltpu.VMEM((2, 4 * EARLY, EROWS, 512), jnp.bfloat16),
+            pltpu.VMEM((2, 4 * EARLY, EROWS, 512), jnp.bfloat16),
+            pltpu.VMEM((2, 2, 512, 256), jnp.float32),
+            pltpu.VMEM((2, 2, 512, 256), jnp.bfloat16),
+            pltpu.VMEM((EARLY, 2, 512, 256), jnp.bfloat16),
+            pltpu.VMEM((2, 2, 512, 128), jnp.float32),
+            pltpu.VMEM((2, 2, 512, 128), jnp.bfloat16),
             dma((SLOTS,)), dma((SLOTS,)), dma((SLOTS,)), dma((SLOTS,)), dma((SLOTS,)),
             dma((10, UNITS)), dma((10, UNITS)), dma((2,)), dma((2,)), dma((2, 2, 2)), dma((UNITS, 2, 2)),
             dma((2, 2, 2)), dma((2, 2)), dma((CHUNKS, 2)), dma((2, 2)), dma((CHUNKS, 2)), dma((2, 2)),
+            dma((2, 2, 2)), dma((2, 2)), dma((EARLY, 2)), dma((2, 2)), dma((EARLY, 2)), dma((2, 2)),
         ],
         compiler_params=pltpu.CompilerParams(
             collective_id=0, has_side_effects=True, vmem_limit_bytes=60 << 20

time: 281 us -> 267 us (0.950)
  Pallas kernels: 272 us -> 258 us
    pallas_call x1, Pallas kernels: 272 us -> 258 us  [per_device(): pl.pallas_call(gradients, name='gradients', out_shape=(jax.ShapeDtypeStru...]
where the time goes in v4:
time: 267 us
  Pallas kernels  258 us (97%)
  other arithmetic  8.8 us (3%)
    pallas_call x1, Pallas kernels, per_device(): pl.pallas_call(gradients, name='gradients', out_shape=(jax.ShapeDtypeStru...  258 us
    add x1, other arithmetic, per_device(): return own_sum + peer_sum.astype(jnp.float32)  8.8 us

profile of v4, /device:TPU:0, one launch (start us, length us, event | category | flops | bytes accessed | tf_op | source)
XLA Modules:
  0.0 266.9 jit_solution(9252401356655613042)
XLA Ops:
  0.0 258.1 %gradients.1 = (f32[16,1024,128]{2,1,0:T(8,128)}, bf16[16,1024,128]{2,1,0:T(8,128)(2,1)}, bf16[10,2,512,512]{3,2,1,0:T(8,128)(2,1)}, bf16[10,2,512,512]{3,2,1,0:T(8,128)(2,1)}, bf16[5,1024,1024]{2,1,0:T(8,128)(2,1)}) custom-call(s32[16]{0:T(128)} %code.1, s32[3,17]{1,0:T(4,128)} %bounds.1, s32[3]{0:T(128)} %micro.1, bf16[5,1024,256]{2,1,0:T(8,128)(2,1)} %bitcast.3, ...), custom_call_target="tpu_custom_call" | custom-call | tf_op jit(solution)/shard_map/gradients/pallas_call | solution.py:487
  258.1 8.8 %convert_add_fusion = f32[16,1024,128]{2,1,0:T(8,128)} fusion(f32[16,1024,128]{2,1,0:T(8,128)} %get-tuple-element.7, bf16[16,1024,128]{2,1,0:T(8,128)(2,1)} %get-tuple-element.8), kind=kLoop, calls=%fused_computation | loop fusion | flops 4194304 | bytes 20971520 | tf_op jit(solution)/shard_map/add | solution.py:529

commit v5 on v4

--- a/solution.py
+++ b/solution.py
@@ -14,7 +14,9 @@
 ROWS = 1024
 WIDTH = 1024
 LAYERS = 16
-CHUNKS = 16
+CHUNKS = 32
+BUFFERS = 4
+DELAY = 3
 SPLIT = 176
 EARLY = 3
 LATE = LAYERS - EARLY
@@ -59,7 +61,6 @@
     peer_y = device(1 - yh, x, c, yl, z)
     ld = (ld_even, ld_odd)
     le = (le_even, le_odd)
-    greet((mate, ypeer, zplus, zminus, peer_a, peer_b, peer_y))
     turn = 1 + 2 * (x % 2)
 
     def column(yy, zz):
@@ -125,10 +126,23 @@
             device_id=(peer_a, peer_b)[h], device_id_type=MESH,
         )
 
+    def mask_own(s):
+        own_column = pl.ds(column(yl, z), 128)
+        limit = jnp.where(s % 2 == 0, limits[0], limits[1])
+        live = (lax.broadcasted_iota(jnp.int32, (ROWS, 128), 0) < limit).astype(jnp.float32)
+        cbuf[s, :, own_column] = (cbuf[s, :, own_column].astype(jnp.float32) * live).astype(jnp.bfloat16)
+
+    own_c(0).start()
+    load_own(0).start()
+    own_c(0).wait()
+    mask_own(0)
+    greet((mate, ypeer, zplus, zminus, peer_a, peer_b, peer_y))
+    for kind in (0, 1, 2):
+        message(kind, 0).start()
     for j in range(SLOTS):
-        own_c(j).start()
+        if j > 0:
+            own_c(j).start()
         mate_c(j).start()
-    load_own(0).start()
     for j in range(SLOTS):
         mate_a(j).start()
 
@@ -276,7 +290,7 @@
 
     @pl.loop(0, UNITS + 1)
     def _(it):
-        @pl.when(it < UNITS)
+        @pl.when((it >= 1) & (it < UNITS))
         def _():
             @pl.when(it % 2 == 0)
             def _():
@@ -286,10 +300,7 @@
             def _():
                 mate_c(it // 2).wait_recv()
 
-            own_column = pl.ds(column(yl, z), 128)
-            limit = jnp.where(it % 2 == 0, limits[0], limits[1])
-            live = (lax.broadcasted_iota(jnp.int32, (ROWS, 128), 0) < limit).astype(jnp.float32)
-            cbuf[it, :, own_column] = (cbuf[it, :, own_column].astype(jnp.float32) * live).astype(jnp.bfloat16)
+            mask_own(it)
             for kind in (0, 1, 2):
                 message(kind, it).start()
 
@@ -373,29 +384,29 @@
                 for load in loads(0, 0):
                     load.start()
 
-        else:
+        if b == (CHUNKS // 2 - 1) % BUFFERS:
             @pl.when(n == CHUNKS // 2 - 1)
             def _():
                 arrived(1)
 
         @pl.when(n + 1 < CHUNKS)
         def _():
-            for load in loads(n + 1, 1 - b):
+            for load in loads(n + 1, 1 - b % 2):
                 load.start()
 
-        for load in loads(n, b):
+        for load in loads(n, b % 2):
             load.wait()
         for h in range(2):
-            @pl.when(n >= 2)
-            def _():
-                send_x(n - 2, b, h).wait_send()
+            @pl.when(n >= BUFFERS)
+            def _():
+                send_x(n - BUFFERS, b, h).wait_send()
 
             @pl.loop(0, LATE)
             def _(layer):
                 total = None
                 for q in range(4):
                     at = (h * LAYERS + EARLY + layer) * 4 + q
-                    term = ld[b][h, slot_of[at]].astype(jnp.float32) * weight_of[at]
+                    term = ld[b % 2][h, slot_of[at]].astype(jnp.float32) * weight_of[at]
                     total = term if total is None else total + term
                 p2k[b, h, layer] = total[:, 0:256]
                 p2s[b, h, layer] = total[:, 256:512].astype(jnp.bfloat16)
@@ -403,11 +414,13 @@
             send_x(n, b, h).start()
 
     def second(n, b):
+        d = b % 2
+
         @pl.when(n >= 2)
         def _():
             for h in range(2):
-                send_y(n - 2, b, h).wait_send()
-                store(n - 2, b, h).wait()
+                send_y(n - 2, d, h).wait_send()
+                store(n - 2, d, h).wait()
 
         for h in range(2):
             send_x(n, b, h).wait_recv()
@@ -415,35 +428,35 @@
             @pl.loop(0, LATE)
             def _(layer):
                 total = p2k[b, h, layer] + p2r[n, h, layer].astype(jnp.float32)
-                p3k[b, h, layer] = total[:, 0:128]
-                p3s[b, h, layer] = total[:, 128:256].astype(jnp.bfloat16)
-
-            send_y(n, b, h).start()
-            store(n, b, h).start()
-
-    @pl.loop(0, CHUNKS // 2 + 1)
+                p3k[d, h, layer] = total[:, 0:128]
+                p3s[d, h, layer] = total[:, 128:256].astype(jnp.bfloat16)
+
+            send_y(n, d, h).start()
+            store(n, d, h).start()
+
+    @pl.loop(0, CHUNKS // BUFFERS + 1)
     def _(it):
-        @pl.when(it == 1)
-        def _():
-            early_second(EARLY - 1)
-
-        for b in range(2):
-            n = it * 2 + b
+        for b in range(BUFFERS):
+            n = it * BUFFERS + b
 
             @pl.when(n < CHUNKS)
             def _():
                 first(n, b)
 
-            @pl.when((n >= 1) & (n < CHUNKS + 1))
-            def _():
-                second(n - 1, 1 - b)
-
+            if b == 1:
+                pl.when(it == 0)(functools.partial(early_second, EARLY - 1))
+
+            @pl.when((n >= DELAY) & (n < CHUNKS + DELAY))
+            def _():
+                second(n - DELAY, (b - DELAY) % BUFFERS)
+
+    for b in range(BUFFERS):
+        for h in range(2):
+            send_x(CHUNKS - BUFFERS + b, b, h).wait_send()
     for b in range(2):
-        n = CHUNKS - 2 + b
-        for h in range(2):
-            send_x(n, b, h).wait_send()
-            send_y(n, b, h).wait_send()
-            store(n, b, h).wait()
+        for h in range(2):
+            send_y(CHUNKS - 2 + b, b, h).wait_send()
+            store(CHUNKS - 2 + b, b, h).wait()
 
     for b in range(2):
         for h in range(2):
@@ -503,8 +516,8 @@
             pltpu.VMEM((2, 2, 512, 512), jnp.bfloat16),
             pltpu.VMEM((2, 2 * UNITS, CROWS, 512), jnp.bfloat16),
             pltpu.VMEM((2, 2 * UNITS, CROWS, 512), jnp.bfloat16),
-            pltpu.VMEM((2, 2, LATE, CROWS, 256), jnp.float32),
-            pltpu.VMEM((2, 2, LATE, CROWS, 256), jnp.bfloat16),
+            pltpu.VMEM((BUFFERS, 2, LATE, CROWS, 256), jnp.float32),
+            pltpu.VMEM((BUFFERS, 2, LATE, CROWS, 256), jnp.bfloat16),
             pltpu.VMEM((CHUNKS, 2, LATE, CROWS, 256), jnp.bfloat16),
             pltpu.VMEM((2, 2, LATE, CROWS, 128), jnp.float32),
             pltpu.VMEM((2, 2, LATE, CROWS, 128), jnp.bfloat16),
@@ -519,7 +532,7 @@
             pltpu.VMEM((2, 2, 512, 128), jnp.bfloat16),
             dma((SLOTS,)), dma((SLOTS,)), dma((SLOTS,)), dma((SLOTS,)), dma((SLOTS,)),
             dma((10, UNITS)), dma((10, UNITS)), dma((2,)), dma((2,)), dma((2, 2, 2)), dma((UNITS, 2, 2)),
-            dma((2, 2, 2)), dma((2, 2)), dma((CHUNKS, 2)), dma((2, 2)), dma((CHUNKS, 2)), dma((2, 2)),
+            dma((2, 2, 2)), dma((BUFFERS, 2)), dma((CHUNKS, 2)), dma((2, 2)), dma((CHUNKS, 2)), dma((2, 2)),
             dma((2, 2, 2)), dma((2, 2)), dma((EARLY, 2)), dma((2, 2)), dma((EARLY, 2)), dma((2, 2)),
         ],
         compiler_params=pltpu.CompilerParams(

time: 267 us -> 264 us (0.989)
  Pallas kernels: 258 us -> 255 us
    pallas_call x1, Pallas kernels: 258 us -> 255 us  [per_device(): pl.pallas_call(gradients, name='gradients', out_shape=(jax.ShapeDtypeStru...]
where the time goes in v5:
time: 264 us
  Pallas kernels  255 us (97%)
  other arithmetic  8.8 us (3%)
    pallas_call x1, Pallas kernels, per_device(): pl.pallas_call(gradients, name='gradients', out_shape=(jax.ShapeDtypeStru...  255 us
    add x1, other arithmetic, per_device(): return own_sum + peer_sum.astype(jnp.float32)  8.8 us

profile of v5, /device:TPU:0, one launch (start us, length us, event | category | flops | bytes accessed | tf_op | source)
XLA Modules:
  0.0 263.7 jit_solution(13771870720409682771)
XLA Ops:
  0.0 254.8 %gradients.1 = (f32[16,1024,128]{2,1,0:T(8,128)}, bf16[16,1024,128]{2,1,0:T(8,128)(2,1)}, bf16[10,2,512,512]{3,2,1,0:T(8,128)(2,1)}, bf16[10,2,512,512]{3,2,1,0:T(8,128)(2,1)}, bf16[5,1024,1024]{2,1,0:T(8,128)(2,1)}) custom-call(s32[16]{0:T(128)} %code.1, s32[3,17]{1,0:T(4,128)} %bounds.1, s32[3]{0:T(128)} %micro.1, bf16[5,1024,256]{2,1,0:T(8,128)(2,1)} %bitcast.3, ...), custom_call_target="tpu_custom_call" | custom-call | tf_op jit(solution)/shard_map/gradients/pallas_call | solution.py:500
  254.9 8.8 %convert_add_fusion = f32[16,1024,128]{2,1,0:T(8,128)} fusion(f32[16,1024,128]{2,1,0:T(8,128)} %get-tuple-element.7, bf16[16,1024,128]{2,1,0:T(8,128)(2,1)} %get-tuple-element.8), kind=kLoop, calls=%fused_computation | loop fusion | flops 4194304 | bytes 20971520 | tf_op jit(solution)/shard_map/add | solution.py:542

commit v6 on v5

--- a/solution.py
+++ b/solution.py
@@ -290,20 +290,6 @@
 
     @pl.loop(0, UNITS + 1)
     def _(it):
-        @pl.when((it >= 1) & (it < UNITS))
-        def _():
-            @pl.when(it % 2 == 0)
-            def _():
-                own_c(it // 2).wait()
-
-            @pl.when(it % 2 == 1)
-            def _():
-                mate_c(it // 2).wait_recv()
-
-            mask_own(it)
-            for kind in (0, 1, 2):
-                message(kind, it).start()
-
         @pl.when(it >= 1)
         def _():
             message(5, it - 1).wait_recv()
@@ -327,6 +313,22 @@
             message(2, it).wait_recv()
             message(6, it).start()
             message(9, it).start()
+
+        @pl.when(it + 1 < UNITS)
+        def _():
+            n = it + 1
+
+            @pl.when(n % 2 == 0)
+            def _():
+                own_c(n // 2).wait()
+
+            @pl.when(n % 2 == 1)
+            def _():
+                mate_c(n // 2).wait_recv()
+
+            mask_own(n)
+            for kind in (0, 1, 2):
+                message(kind, n).start()
 
         @pl.when(it >= 1)
         def _():

time: 264 us -> 264 us (level)
  no operation moved by 1% of the time
where the time goes in v6:
time: 264 us; the launch traced here: 263 us
  Pallas kernels  255 us (97%)
  other arithmetic  8.8 us (3%)
    pallas_call x1, Pallas kernels, per_device(): pl.pallas_call(gradients, name='gradients', out_shape=(jax.ShapeDtypeStru...  255 us
    add x1, other arithmetic, per_device(): return own_sum + peer_sum.astype(jnp.float32)  8.8 us

profile of v6, /device:TPU:0, one launch (start us, length us, event | category | flops | bytes accessed | tf_op | source)
XLA Modules:
  0.0 263.4 jit_solution(2022979565555316551)
XLA Ops:
  0.0 254.6 %gradients.1 = (f32[16,1024,128]{2,1,0:T(8,128)}, bf16[16,1024,128]{2,1,0:T(8,128)(2,1)}, bf16[10,2,512,512]{3,2,1,0:T(8,128)(2,1)}, bf16[10,2,512,512]{3,2,1,0:T(8,128)(2,1)}, bf16[5,1024,1024]{2,1,0:T(8,128)(2,1)}) custom-call(s32[16]{0:T(128)} %code.1, s32[3,17]{1,0:T(4,128)} %bounds.1, s32[3]{0:T(128)} %micro.1, bf16[5,1024,256]{2,1,0:T(8,128)(2,1)} %bitcast.3, ...), custom_call_target="tpu_custom_call" | custom-call | tf_op jit(solution)/shard_map/gradients/pallas_call | solution.py:502
  254.6 8.8 %convert_add_fusion = f32[16,1024,128]{2,1,0:T(8,128)} fusion(f32[16,1024,128]{2,1,0:T(8,128)} %get-tuple-element.7, bf16[16,1024,128]{2,1,0:T(8,128)(2,1)} %get-tuple-element.8), kind=kLoop, calls=%fused_computation | loop fusion | flops 4194304 | bytes 20971520 | tf_op jit(solution)/shard_map/add | solution.py:544
